TPU v7x, 32 devices: a whole 2x2x4 slice. The times are simulated.
32 devices in a mesh: dp: 4 (over y, x), gx: 4 (over z), gy: 2 (over core).
Axes of the slice: x: 2, y: 2, z: 4, core: 2. Of those that a mesh axis runs over, the one named last changes fastest.
Arguments:
- hidden_in: bfloat16 [4, 1024, 768], P('dp', 'gx', 'gy'), may hold values from -6 to 6
- encoded: bfloat16 [4, 1024, 768], P('dp', 'gx', 'gy'), may hold values from -6 to 6
- doc_ids: int32 [4, 1024], P('dp'), may hold values from 0 to 7, never falling along the last dimension, each value on 1 to 768 neighbouring positions
- buckets: int32 [1024], replicated, may hold values from 0 to 31, as said below
- rel_table: float32 [32, 12], replicated, may hold values from -6 to 6
- norm_gains: float32 [3, 768], replicated, may hold values from 0.5 to 1.5
- self_q: bfloat16 [768, 768], P('gy', 'gx'), may hold values from -0.02734375 to 0.02734375
- self_k: bfloat16 [768, 768], P('gy', 'gx'), may hold values from -0.21875 to 0.21875
- self_v: bfloat16 [768, 768], P('gy', 'gx'), may hold values from -0.21875 to 0.21875
- self_out: bfloat16 [768, 768], P('gx', 'gy'), may hold values from -1.75 to 1.75
- cross_q: bfloat16 [768, 768], P('gy', 'gx'), may hold values from -0.02734375 to 0.02734375
- cross_k: bfloat16 [768, 768], P('gy', 'gx'), may hold values from -0.21875 to 0.21875
- cross_v: bfloat16 [768, 768], P('gy', 'gx'), may hold values from -0.21875 to 0.21875
- cross_out: bfloat16 [768, 768], P('gx', 'gy'), may hold values from -3.5 to 3.5
- ff_gate: bfloat16 [768, 2048], P('gy', 'gx'), may hold values from -0.21875 to 0.21875
- ff_up: bfloat16 [768, 2048], P('gy', 'gx'), may hold values from -0.21875 to 0.21875
- ff_down: bfloat16 [2048, 768], P('gx', 'gy'), may hold values from -0.125 to 0.125
- grad_out: bfloat16 [4, 1024, 768], P('dp', 'gx', 'gy'), may hold values from -6 to 6
Outputs:
- layer_out: bfloat16 [4, 1024, 768], P('dp', 'gx', 'gy')
- grad_hidden: float32 [4, 1024, 768], P('dp', 'gx', 'gy')
- grad_encoded: float32 [4, 1024, 768], P('dp', 'gx', 'gy')
- grad_gains: float32 [3, 768], replicated
- grad_rel: float32 [32, 12], replicated
- grad_self_q: float32 [768, 768], P('gy', 'gx')
- grad_self_k: float32 [768, 768], P('gy', 'gx')
- grad_self_v: float32 [768, 768], P('gy', 'gx')
- grad_self_out: float32 [768, 768], P('gx', 'gy')
- grad_cross_q: float32 [768, 768], P('gy', 'gx')
- grad_cross_k: float32 [768, 768], P('gy', 'gx')
- grad_cross_v: float32 [768, 768], P('gy', 'gx')
- grad_cross_out: float32 [768, 768], P('gx', 'gy')
- grad_ff_gate: float32 [768, 2048], P('gy', 'gx')
- up_projection_gradient: float32 [768, 2048], P('gy', 'gx')
- grad_ff_down: float32 [2048, 768], P('gx', 'gy')
Inputs may be any that keep to these rules, and one draw needn't show every extreme that they name: `buckets`: nondecreasing in the distance, 0 at distance 0 and 31 at distance 1024 - 1. `doc_ids`: document numbers never fall along a sequence; each of the 8 documents has 1 to 768 tokens and one has exactly that many.
All inputs are finite; a program needn't handle non-finite values.
Results may differ from a plain program's by a relative error of at most 0.023.
Values may be sent and summed in bfloat16 or wider, within the bound.
A program may use at most 128 MiB of HBM per device.

v0:
```python
import jax
import jax.numpy as jnp
from jax import lax
from jax.sharding import PartitionSpec as P

DH = 64


epsilon = 1e-06
masked_score = -1000000000.0


def rows_over_x(stacked):
    return lax.all_gather(stacked, "gx", axis=2, tiled=True)


def rows_over_y(stacked):
    return lax.all_gather(stacked, "gy", axis=2, tiled=True)


def sums_over_y(stacked):
    return lax.psum_scatter(stacked, "gy", scatter_dimension=2, tiled=True)


def sums_over_x(stacked):
    return lax.psum_scatter(stacked, "gx", scatter_dimension=2, tiled=True)


def feature_total(partial_value):
    return lax.psum(partial_value, "gy")


def project_rows(collected_shards, weight_list):
    return jnp.stack(
        [
            jnp.einsum(
                "iwm,mv->iwv", collected_shards, weight_matrix, preferred_element_type=jnp.float32
            )
            for weight_matrix in weight_list
        ]
    )


def input_grads(gradient_row_block, weight_list):
    reduced_total = jnp.einsum(
        "ohz,nz->ohn", gradient_row_block[0], weight_list[0], preferred_element_type=jnp.float32
    )
    for shard_member in range(1, len(weight_list)):
        reduced_total = reduced_total + jnp.einsum(
            "ohz,nz->ohn",
            gradient_row_block[shard_member],
            weight_list[shard_member],
            preferred_element_type=jnp.float32,
        )
    return reduced_total


def project_own(collected_shards, blocks):
    return sums_over_y(project_rows(collected_shards, blocks))


def back_own(gradient_row_block, blocks):
    return sums_over_y(input_grads(gradient_row_block[None], blocks)[None])[0]


def weight_grad(collected_shards, gradient_row_block):
    return jnp.einsum(
        "tkv,tkb->vb", collected_shards, gradient_row_block, preferred_element_type=jnp.float32
    )


def norm_forward(stream, gain_part, feature_count):
    squares = feature_total(jnp.sum(stream * stream, axis=-1))
    inv_root = lax.rsqrt(squares / feature_count + epsilon)
    normal = stream * inv_root[..., None]
    return (normal * gain_part, normal, inv_root)


def norm_backward(grad_normed, normal, inv_root, gain_part, feature_count):
    gain_grad = jnp.sum(grad_normed * normal, axis=(0, 1))
    scaled = grad_normed * gain_part
    inner_sum = feature_total(jnp.sum(scaled * normal, axis=-1)) / feature_count
    return (inv_root[..., None] * (scaled - normal * inner_sum[..., None]), gain_grad)


def glu_piece(gate, up_part):
    return jax.nn.gelu(gate, approximate=True) * up_part


def split_heads(block):
    return block.reshape(block.shape[0], block.shape[1] // DH, DH)


def distance_grid(by_distance, first_row, row_count):
    head_count, col_count = by_distance.shape
    span = col_count + row_count - 1
    padded = jnp.concatenate([jnp.zeros((head_count, col_count), jnp.float32), by_distance], axis=1)
    reverse = padded[:, ::-1]
    hankel = lax.dynamic_slice_in_dim(reverse, col_count - first_row - row_count, span, 1)
    repeated = jnp.tile(hankel, (1, row_count + 1))[:, : row_count * (span + 1)]
    matrix = repeated.reshape(head_count, row_count, span + 1)[:, :, :col_count]
    return matrix[:, ::-1, :]


def diagonal_sums(matrix, first_row):
    head_count, row_count, col_count = matrix.shape
    span = col_count + row_count - 1
    flipped = matrix[:, ::-1, :]
    padded = jnp.pad(flipped, ((0, 0), (0, 0), (0, row_count)))
    flattened = jnp.pad(
        padded.reshape(head_count, row_count * (span + 1)), ((0, 0), (0, span - row_count))
    )
    by_sum = jnp.sum(flattened.reshape(head_count, row_count + 1, span), axis=1)
    reverse = jnp.concatenate(
        [by_sum[:, ::-1], jnp.zeros((head_count, col_count), jnp.float32)], axis=1
    )
    return lax.dynamic_slice_in_dim(reverse, col_count - 1 - first_row, col_count, 1)


def score_grid(queries, key_rows, bias, allowed):
    scores = jnp.einsum(
        "qhd,khd->hqk",
        split_heads(queries),
        split_heads(key_rows),
        preferred_element_type=jnp.float32,
    )
    if bias is not None:
        scores = scores + bias
    if allowed is not None:
        scores = jnp.where(allowed[None], scores, masked_score)
    return scores


def attend(queries, key_rows, value_rows, bias, allowed):
    scores = score_grid(queries, key_rows, bias, allowed)
    row_top = jnp.max(scores, axis=-1, keepdims=True)
    exponent = jnp.exp(scores - row_top)
    row_total_sum = jnp.sum(exponent, axis=-1, keepdims=True)
    weights_low = (exponent / row_total_sum).astype(jnp.bfloat16)
    context = jnp.einsum(
        "hqk,khd->qhd", weights_low, split_heads(value_rows), preferred_element_type=jnp.float32
    )
    return (
        context.reshape(queries.shape).astype(jnp.bfloat16),
        (row_top + jnp.log(row_total_sum))[..., 0],
    )


def attend_back(queries, key_rows, value_rows, bias, allowed, logsum, grad_context):
    scores = score_grid(queries, key_rows, bias, allowed)
    chances = jnp.exp(scores - logsum[..., None])
    grad_heads = split_heads(grad_context)
    grad_chances = jnp.einsum(
        "qhd,khd->hqk", grad_heads, split_heads(value_rows), preferred_element_type=jnp.float32
    )
    grad_values = jnp.einsum(
        "hqk,qhd->khd", chances.astype(jnp.bfloat16), grad_heads, preferred_element_type=jnp.float32
    )
    inner_sum = jnp.sum(grad_chances * chances, axis=-1, keepdims=True)
    grad_scores = (chances * (grad_chances - inner_sum)).astype(jnp.bfloat16)
    grad_queries = jnp.einsum(
        "hqk,khd->qhd", grad_scores, split_heads(key_rows), preferred_element_type=jnp.float32
    )
    grad_keys = jnp.einsum(
        "hqk,qhd->khd", grad_scores, split_heads(queries), preferred_element_type=jnp.float32
    )
    return (
        grad_queries.reshape(queries.shape),
        grad_keys.reshape(key_rows.shape),
        grad_values.reshape(value_rows.shape),
        grad_scores,
    )


def body(
    hidden_in,
    encoded,
    doc_ids,
    buckets,
    rel_table,
    norm_gains,
    self_q,
    self_k,
    self_v,
    self_out,
    cross_q,
    cross_k,
    cross_v,
    cross_out,
    ff_gate,
    ff_up,
    ff_down,
    grad_out,
):
    model_width = norm_gains.shape[1]
    part_width = hidden_in.shape[2]
    seq_len = doc_ids.shape[1]
    query_count = seq_len // lax.axis_size("gy")
    head_part = self_q.shape[1] // DH
    row_index = lax.axis_index("gy")
    col_index = lax.axis_index("gx")
    first_row = row_index * query_count
    gains_part = lax.dynamic_slice_in_dim(norm_gains, row_index * part_width, part_width, 1)
    table_part = lax.dynamic_slice_in_dim(rel_table, col_index * head_part, head_part, 1)
    bucket_hot = (
        buckets[:, None] == jnp.arange(rel_table.shape[0], dtype=jnp.int32)[None, :]
    ).astype(jnp.float32)
    by_distance = jnp.dot(bucket_hot, table_part, precision=lax.Precision.HIGHEST).T
    bias_grid = distance_grid(by_distance, first_row, query_count)
    query_pos = first_row + jnp.arange(query_count, dtype=jnp.int32)
    causal = jnp.arange(seq_len, dtype=jnp.int32)[None, :] <= query_pos[:, None]
    query_docs = lax.dynamic_slice_in_dim(doc_ids, first_row, query_count, 1)

    def self_allowed(own_docs, all_docs):
        return causal & (own_docs[:, None] == all_docs[None, :])

    stream_in = hidden_in.astype(jnp.float32)
    normed_one, plain_one, root_one = norm_forward(stream_in, gains_part[0], model_width)
    low_one = normed_one.astype(jnp.bfloat16)
    rows_one = rows_over_x(low_one[None])[0]
    self_proj = project_own(rows_one, (self_q, self_k, self_v)).astype(jnp.bfloat16)
    self_keys = rows_over_y(self_proj[1:])

    def self_forward(members):
        queries, key_rows, value_rows, own_docs, all_docs = members
        return attend(queries, key_rows, value_rows, bias_grid, self_allowed(own_docs, all_docs))

    self_context, self_logsum = lax.map(
        self_forward, (self_proj[0], self_keys[0], self_keys[1], query_docs, doc_ids)
    )
    context_rows = rows_over_y(self_context[None])[0]
    stream_one = stream_in + sums_over_x(project_rows(context_rows, (self_out,)))[0]
    normed_two, plain_two, root_two = norm_forward(stream_one, gains_part[1], model_width)
    low_two = normed_two.astype(jnp.bfloat16)
    rows_two = rows_over_x(low_two[None])[0]
    enc_rows = rows_over_x(encoded[None])[0]
    cross_query = project_own(rows_two, (cross_q,)).astype(jnp.bfloat16)[0]
    cross_proj = project_own(enc_rows, (cross_k, cross_v)).astype(jnp.bfloat16)
    cross_keys = rows_over_y(cross_proj)

    def cross_forward(members):
        queries, key_rows, value_rows = members
        return attend(queries, key_rows, value_rows, None, None)

    cross_context, cross_logsum = lax.map(
        cross_forward, (cross_query, cross_keys[0], cross_keys[1])
    )
    cross_rows = rows_over_y(cross_context[None])[0]
    stream_two = stream_one + sums_over_x(project_rows(cross_rows, (cross_out,)))[0]
    normed_three, plain_three, root_three = norm_forward(stream_two, gains_part[2], model_width)
    low_three = normed_three.astype(jnp.bfloat16)
    rows_three = rows_over_x(low_three[None])[0]
    gate_up = project_own(rows_three, (ff_gate, ff_up))
    hidden_float, glu_pull = jax.vjp(glu_piece, gate_up[0], gate_up[1])
    hidden_low = hidden_float.astype(jnp.bfloat16)
    hidden_rows = rows_over_y(hidden_low[None])[0]
    layer_out = (stream_two + sums_over_x(project_rows(hidden_rows, (ff_down,)))[0]).astype(
        jnp.bfloat16
    )
    down_rows = rows_over_x(grad_out[None])[0]
    grad_ff_down = weight_grad(hidden_rows, down_rows)
    grad_hidden_part = back_own(down_rows, (ff_down,))
    grad_gate, grad_up = glu_pull(grad_hidden_part)
    glu_rows = rows_over_y(jnp.stack([grad_gate, grad_up]).astype(jnp.bfloat16))
    grad_ff_gate = weight_grad(rows_three, glu_rows[0])
    up_projection_gradient = weight_grad(rows_three, glu_rows[1])
    ff_grads = (grad_ff_gate, up_projection_gradient, grad_ff_down)
    grad_norm_three = sums_over_x(input_grads(glu_rows, (ff_gate, ff_up))[None])[0]
    back_three, gain_three = norm_backward(
        grad_norm_three, plain_three, root_three, gains_part[2], model_width
    )
    grad_two = grad_out.astype(jnp.float32) + back_three
    cross_out_rows = rows_over_x(grad_two.astype(jnp.bfloat16)[None])[0]
    grad_cross_out = weight_grad(cross_rows, cross_out_rows)
    grad_cross_context = back_own(cross_out_rows, (cross_out,)).astype(jnp.bfloat16)

    def cross_backward(members):
        queries, key_rows, value_rows, logsum, grad_context = members
        return attend_back(queries, key_rows, value_rows, None, None, logsum, grad_context)[:3]

    cross_query_grad, cross_key_grad, cross_value_grad = lax.map(
        cross_backward,
        (cross_query, cross_keys[0], cross_keys[1], cross_logsum, grad_cross_context),
    )
    cross_pair_grad = sums_over_y(jnp.stack([cross_key_grad, cross_value_grad])).astype(
        jnp.bfloat16
    )
    cross_query_rows = rows_over_y(cross_query_grad.astype(jnp.bfloat16)[None])
    cross_pair_rows = rows_over_y(cross_pair_grad)
    grad_cross_q = weight_grad(rows_two, cross_query_rows[0])
    grad_cross_k = weight_grad(enc_rows, cross_pair_rows[0])
    grad_cross_v = weight_grad(enc_rows, cross_pair_rows[1])
    cross_grads = (grad_cross_q, grad_cross_k, grad_cross_v, grad_cross_out)
    grad_norm_two = sums_over_x(input_grads(cross_query_rows, (cross_q,))[None])[0]
    grad_encoded = sums_over_x(input_grads(cross_pair_rows, (cross_k, cross_v))[None])[0]
    back_two, gain_two = norm_backward(
        grad_norm_two, plain_two, root_two, gains_part[1], model_width
    )
    grad_one = grad_two + back_two
    self_out_rows = rows_over_x(grad_one.astype(jnp.bfloat16)[None])[0]
    grad_self_out = weight_grad(context_rows, self_out_rows)
    grad_self_context = back_own(self_out_rows, (self_out,)).astype(jnp.bfloat16)

    def self_backward(members):
        queries, key_rows, value_rows, own_docs, all_docs, logsum, grad_context = members
        grad_queries, grad_keys, grad_values, grad_scores = attend_back(
            queries,
            key_rows,
            value_rows,
            bias_grid,
            self_allowed(own_docs, all_docs),
            logsum,
            grad_context,
        )
        return (
            grad_queries,
            grad_keys,
            grad_values,
            diagonal_sums(grad_scores.astype(jnp.float32), first_row),
        )

    self_query_grad, self_key_grad, self_value_grad, distance_grad = lax.map(
        self_backward,
        (
            self_proj[0],
            self_keys[0],
            self_keys[1],
            query_docs,
            doc_ids,
            self_logsum,
            grad_self_context,
        ),
    )
    self_pair_grad = sums_over_y(jnp.stack([self_key_grad, self_value_grad])).astype(jnp.bfloat16)
    self_grad_rows = rows_over_y(
        jnp.concatenate([self_query_grad.astype(jnp.bfloat16)[None], self_pair_grad])
    )
    grad_self_q = weight_grad(rows_one, self_grad_rows[0])
    grad_self_k = weight_grad(rows_one, self_grad_rows[1])
    grad_self_v = weight_grad(rows_one, self_grad_rows[2])
    self_grads = (grad_self_q, grad_self_k, grad_self_v, grad_self_out)
    grad_norm_one = sums_over_x(input_grads(self_grad_rows, (self_q, self_k, self_v))[None])[0]
    back_one, gain_one = norm_backward(
        grad_norm_one, plain_one, root_one, gains_part[0], model_width
    )
    grad_hidden = grad_one + back_one
    table_grad = jnp.dot(
        bucket_hot.T, jnp.sum(distance_grad, axis=0).T, precision=lax.Precision.HIGHEST
    )
    rel_full = lax.dynamic_update_slice(
        jnp.zeros(rel_table.shape, jnp.float32), table_grad, (0, col_index * head_part)
    )
    gain_full = lax.dynamic_update_slice(
        jnp.zeros(norm_gains.shape, jnp.float32),
        jnp.stack([gain_one, gain_two, gain_three]),
        (0, row_index * part_width),
    )
    grad_gains, grad_rel = lax.psum((gain_full, rel_full), ("dp", "gx", "gy"))
    weight_grads = (
        lax.psum(self_grads[0].astype(jnp.bfloat16), "dp").astype(jnp.float32),
        lax.psum(self_grads[1].astype(jnp.bfloat16), "dp").astype(jnp.float32),
        lax.psum(self_grads[2].astype(jnp.bfloat16), "dp").astype(jnp.float32),
        lax.psum(self_grads[3].astype(jnp.bfloat16), "dp").astype(jnp.float32),
        lax.psum(cross_grads[0].astype(jnp.bfloat16), "dp").astype(jnp.float32),
        lax.psum(cross_grads[1].astype(jnp.bfloat16), "dp").astype(jnp.float32),
        lax.psum(cross_grads[2].astype(jnp.bfloat16), "dp").astype(jnp.float32),
        lax.psum(cross_grads[3].astype(jnp.bfloat16), "dp").astype(jnp.float32),
        lax.psum(ff_grads[0].astype(jnp.bfloat16), "dp").astype(jnp.float32),
        lax.psum(ff_grads[1].astype(jnp.bfloat16), "dp").astype(jnp.float32),
        lax.psum(ff_grads[2].astype(jnp.bfloat16), "dp").astype(jnp.float32),
    )
    return (
        layer_out,
        grad_hidden,
        grad_encoded,
        grad_gains,
        grad_rel,
        weight_grads[0],
        weight_grads[1],
        weight_grads[2],
        weight_grads[3],
        weight_grads[4],
        weight_grads[5],
        weight_grads[6],
        weight_grads[7],
        weight_grads[8],
        weight_grads[9],
        weight_grads[10],
    )


def solution(mesh):
    placed = (
        P("dp", "gx", "gy"),
        P("dp", "gx", "gy"),
        P("dp", None),
        P(),
        P(),
        P(),
        P("gy", "gx"),
        P("gy", "gx"),
        P("gy", "gx"),
        P("gx", "gy"),
        P("gy", "gx"),
        P("gy", "gx"),
        P("gy", "gx"),
        P("gx", "gy"),
        P("gy", "gx"),
        P("gy", "gx"),
        P("gx", "gy"),
        P("dp", "gx", "gy"),
    )
    return jax.shard_map(
        body,
        mesh=mesh,
        in_specs=placed,
        out_specs=(
            P("dp", "gx", "gy"),
            P("dp", "gx", "gy"),
            P("dp", "gx", "gy"),
            P(),
            P(),
            P("gy", "gx"),
            P("gy", "gx"),
            P("gy", "gx"),
            P("gx", "gy"),
            P("gy", "gx"),
            P("gy", "gx"),
            P("gy", "gx"),
            P("gx", "gy"),
            P("gy", "gx"),
            P("gy", "gx"),
            P("gx", "gy"),
        ),
        check_vma=False,
    )
```

profile of v0, /device:TPU:0, one launch (start us, length us, event | category | flops | bytes accessed | tf_op | source)
XLA Modules:
  0.0 771.7 jit_solution(12168419067841596994)
XLA Ops:
  8.4 2.6 psum.133
  13.0 21.1 %all-gather = bf16[1,1024,384]{2,1,0:T(8,128)(2,1)S(1)} all-gather(bf16[1,256,384]{2,1,0:T(8,128)(2,1)S(1)} %fusion.55), channel_id=2, replica_groups=mesh['dp'=4,'gx'=4,'gy'=2] {'gx'}, dimensions={1}, use_global_device_ids=true | all-gather | bytes 983040 | tf_op jit(solution)/shard_map/all_gather | solution.py:14
  40.9 5.3 tile.4
  46.2 15.5 %reshape.714 = f32[2362365]{0:T(1024)} reshape(f32[3,513,1535]{2,1,0:T(8,128)} %tile.4) | data formatting | bytes 18898920
  61.7 14.1 %tile.10 = f32[3,787455]{1,0:T(4,128)} reshape(f32[2362365]{0:T(1024)} %reshape.714) | data formatting | bytes 18898920 | tf_op jit(solution)/shard_map/tile | solution.py:100
  75.8 4.6 slice-done.4
  80.4 6.5 copy.37
  86.9 6.5 slice.100
  93.4 48.5 %rev.15 = f32[3,512,1024]{2,1,0:T(8,128)} reverse(f32[3,512,1024]{2,1,0:T(8,128)} %slice.100), dimensions={1} | reverse | bytes 12582912 | tf_op jit(solution)/shard_map/rev | solution.py:102
  143.8 2.4 all_gather.49
  146.3 4.3 fusion.84
  154.9 2.2 all_gather.50
  159.6 26.2 %all-gather.1 = bf16[1,1024,384]{2,1,0:T(8,128)(2,1)S(1)} all-gather(bf16[1,256,384]{2,1,0:T(8,128)(2,1)S(1)} %copy-done.56), channel_id=3, replica_groups=mesh['dp'=4,'gx'=4,'gy'=2] {'gx'}, dimensions={1}, use_global_device_ids=true | all-gather | bytes 983040 | tf_op jit(solution)/shard_map/all_gather | solution.py:14
  188.5 14.3 %reduce-scatter.19.cloned.1.call-done = f32[1,1,256,384]{3,2,1,0:T(8,128)} async-done(((f32[1,1,1024,384]{3,2,1,0:T(8,128)}), f32[1,1,256,384]{3,2,1,0:T(8,128)}) %reduce-scatter.19.cloned.1.call-update) | async-done | bytes 393232 | tf_op jit(solution)/shard_map/reduce_scatter | solution.py:26
  204.0 2.5 psum.134
  206.6 19.3 %all-gather.2 = bf16[1,1024,384]{2,1,0:T(8,128)(2,1)S(1)} all-gather(bf16[1,256,384]{2,1,0:T(8,128)(2,1)S(1)} %multiply_convert_fusion.5), channel_id=4, replica_groups=mesh['dp'=4,'gx'=4,'gy'=2] {'gx'}, dimensions={1}, use_global_device_ids=true | all-gather | bytes 983040 | tf_op jit(solution)/shard_map/all_gather | solution.py:14
  229.4 2.5 all_gather.52
  232.0 4.3 reduce-scatter.23.cloned.1.call-done
  242.8 2.2 all_gather.54
  247.5 28.0 %all-gather.4 = bf16[1,1024,384]{2,1,0:T(8,128)(2,1)S(1)} all-gather(bf16[1,256,384]{2,1,0:T(8,128)(2,1)S(1)} %copy-done.33), channel_id=6, replica_groups=mesh['dp'=4,'gx'=4,'gy'=2] {'gx'}, dimensions={1}, use_global_device_ids=true | all-gather | bytes 983040 | tf_op jit(solution)/shard_map/all_gather | solution.py:14
  278.6 13.3 %reduce-scatter.25.cloned.1.call-done = f32[1,1,256,384]{3,2,1,0:T(8,128)} async-done(((f32[1,1,1024,384]{3,2,1,0:T(8,128)}), f32[1,1,256,384]{3,2,1,0:T(8,128)}) %reduce-scatter.25.cloned.1.call-update) | async-done | bytes 393232 | tf_op jit(solution)/shard_map/reduce_scatter | solution.py:26
  293.0 2.5 psum.135
  295.6 19.9 %all-gather.3 = bf16[1,1024,384]{2,1,0:T(8,128)(2,1)S(1)} all-gather(bf16[1,256,384]{2,1,0:T(8,128)(2,1)S(1)} %multiply_convert_fusion.4), channel_id=5, replica_groups=mesh['dp'=4,'gx'=4,'gy'=2] {'gx'}, dimensions={1}, use_global_device_ids=true | all-gather | bytes 983040 | tf_op jit(solution)/shard_map/all_gather | solution.py:14
  317.1 2.5 pad_maximum_fusion
  319.7 11.8 %reduce-scatter.27.cloned.1.call-done = f32[2,1,512,512]{3,2,1,0:T(8,128)} async-done(((f32[2,1,1024,512]{3,2,1,0:T(8,128)}), f32[2,1,512,512]{3,2,1,0:T(8,128)}) %reduce-scatter.27.cloned.1.call-update) | async-done | bytes 2097168 | tf_op jit(solution)/shard_map/reduce_scatter | solution.py:22
  331.5 3.5 fusion.23
  336.1 11.9 %all-gather.13.cloned.1.call-done = bf16[2,1,1024,512]{3,2,1,0:T(8,128)(2,1)} async-done(((bf16[2,1,512,512]{3,2,1,0:T(8,128)(2,1)}), bf16[2,1,1024,512]{3,2,1,0:T(8,128)(2,1)}) %all-gather.13.cloned.1.call-update) | async-done | bytes 2097168 | tf_op jit(solution)/shard_map/all_gather | solution.py:18
  352.2 36.6 %reduce-scatter.33.cloned.1.call-done = f32[1,1,256,384]{3,2,1,0:T(8,128)} async-done(((f32[1,1,1024,384]{3,2,1,0:T(8,128)}), f32[1,1,256,384]{3,2,1,0:T(8,128)}) %reduce-scatter.33.cloned.1.call-update) | async-done | bytes 393232 | tf_op jit(solution)/shard_map/reduce_scatter | solution.py:26
  389.9 2.5 psum.136
  393.6 17.9 %all-gather.5 = bf16[1,1024,384]{2,1,0:T(8,128)(2,1)S(1)} all-gather(bf16[1,256,384]{2,1,0:T(8,128)(2,1)S(1)} %fusion.80), channel_id=7, replica_groups=mesh['dp'=4,'gx'=4,'gy'=2] {'gx'}, dimensions={1}, use_global_device_ids=true | all-gather | bytes 983040 | tf_op jit(solution)/shard_map/all_gather | solution.py:14
  414.5 7.1 reduce-scatter.35.cloned.1.call-done
  422.7 3.9 multiply_reduce_fusion.1
  431.6 2.4 all_gather.60
  436.1 3.1 convolution_bitcast_fusion.4
  439.3 33.6 %reduce-scatter.37.cloned.1.call-done = f32[1,1,256,384]{3,2,1,0:T(8,128)} async-done(((f32[1,1,1024,384]{3,2,1,0:T(8,128)}), f32[1,1,256,384]{3,2,1,0:T(8,128)}) %reduce-scatter.37.cloned.1.call-update) | async-done | bytes 393232 | tf_op jit(solution)/shard_map/reduce_scatter | solution.py:26
  474.1 2.5 psum.137
  476.6 32.9 %reduce-scatter.29.cloned.1.call-done = f32[1,1,256,384]{3,2,1,0:T(8,128)} async-done(((f32[1,1,1024,384]{3,2,1,0:T(8,128)}), f32[1,1,256,384]{3,2,1,0:T(8,128)}) %reduce-scatter.29.cloned.1.call-update) | async-done | bytes 393232 | tf_op jit(solution)/shard_map/reduce_scatter | solution.py:26
  509.5 2.1 fusion.81
  511.6 18.1 %all-gather.6 = bf16[1,1024,384]{2,1,0:T(8,128)(2,1)S(1)} all-gather(bf16[1,256,384]{2,1,0:T(8,128)(2,1)S(1)} %get-tuple-element.143), channel_id=8, replica_groups=mesh['dp'=4,'gx'=4,'gy'=2] {'gx'}, dimensions={1}, use_global_device_ids=true | all-gather | bytes 983040 | tf_op jit(solution)/shard_map/all_gather | solution.py:14
  532.0 7.6 reduce-scatter.39.cloned.1.call-done
  540.7 4.1 fusion.4
  544.8 3.9 multiply_reduce_fusion
  552.2 2.6 fusion.87
  554.8 3.9 fusion.6
  560.1 3.1 convolution_convert_fusion
  563.3 2.9 convolution_convert_fusion.1
  573.4 2.4 convolution_convert_fusion.5
  577.1 2.4 all_gather.63
  579.5 2.5 fusion.16
  584.1 2.8 all-gather.15.cloned.1.call-done
  586.9 2.3 convolution_convert_fusion.6
  589.2 2.3 convolution_convert_fusion.7
  591.4 2.3 convolution_convert_fusion.8
  596.9 2.7 add_bitcast_fusion.1
  601.1 2.7 add_bitcast_fusion
  603.9 31.7 %rev.16 = f32[3,512,1024]{2,1,0:T(8,128)} reverse(bf16[3,512,1024]{2,1,0:T(8,128)(2,1)S(1)} %multiply_convert_fusion), dimensions={1} | reverse | bytes 9437184 | tf_op jit(solution)/shard_map/while/body/eval_jaxpr/rev | solution.py:108
  635.5 4.1 pad_bitcast_fusion
  639.6 19.9 %copy.35 = f32[1,3,512,1536]{3,1,2,0:T(4,128)S(1)} copy(f32[1,3,512,1536]{3,2,1,0:T(8,128)S(1)} %pad_bitcast_fusion) | data formatting | bytes 18874368
  659.5 5.0 pad.13
  664.5 14.2 %reshape.716 = f32[2362365]{0:T(1024)} reshape(f32[3,787455]{1,0:T(4,128)} %pad.13) | data formatting | bytes 18898920
  678.7 16.6 %reshape.696 = f32[3,513,1535]{2,1,0:T(8,128)} reshape(f32[2362365]{0:T(1024)} %reshape.716) | data formatting | bytes 18898920 | tf_op jit(solution)/shard_map/while/body/eval_jaxpr/reshape | solution.py:113
  695.3 4.3 reduce_sum.166
  718.0 2.5 psum.138
  720.5 42.2 %all-reduce.4 = (f32[3,768]{1,0:T(4,128)}, f32[32,12]{0,1:T(8,128)}) all-reduce(f32[3,768]{1,0:T(4,128)S(1)} %maximum_dynamic-update-slice_fusion, f32[32,12]{0,1:T(8,128)S(1)} %dynamic_update_slice.34), channel_id=1, replica_groups=mesh['dp'=4,'gx'=4,'gy'=2] {'dp','gx','gy'}, use_global_device_ids=true, to_apply=%region_37.38 | all-reduce | flops 2688 | bytes 21504 | tf_op jit(solution)/shard_map/psum | solution.py:358
  (288 shorter events, 104.3 us)
Async XLA Ops:
  7.2 309.2 %copy-start = (bf16[384,512]{1,0:T(8,128)(2,1)S(1)}, bf16[384,512]{1,0:T(8,128)(2,1)}, u32[]{:S(2)}) copy-start(bf16[384,512]{1,0:T(8,128)(2,1)} %param.32) | copy-start | bytes 1179652
  7.2 28.4 %copy-start.47 = (bf16[384,192]{0,1:T(8,128)(2,1)S(1)}, bf16[384,192]{0,1:T(8,128)(2,1)}, u32[]{:S(2)}) copy-start(bf16[384,192]{0,1:T(8,128)(2,1)} %param.26) | copy-start | bytes 442372
  7.2 28.8 %copy-start.45 = (bf16[384,192]{0,1:T(8,128)(2,1)S(1)}, bf16[384,192]{0,1:T(8,128)(2,1)}, u32[]{:S(2)}) copy-start(bf16[384,192]{0,1:T(8,128)(2,1)} %param.24) | copy-start | bytes 442372
  7.2 135.2 %reduce-scatter.17.cloned.1.call-start = ((), (), s32[]{:S(2)}) async-start(), calls=%async_computation.16 | async-start | bytes 3538944 | tf_op jit(solution)/shard_map/reduce_scatter | solution.py:22
  11.0 25.5 %copy-start.60 = (f32[1,256]{1,0:T(1,128)}, f32[1,256]{1,0:T(1,128)S(1)}, u32[]{:S(2)}) copy-start(f32[1,256]{1,0:T(1,128)S(1)} %add_rsqrt_fusion.2) | copy-start | bytes 3076
  11.9 24.6 %copy-start.58 = (f32[384]{0:T(512)}, f32[384]{0:T(512)S(1)}, u32[]{:S(2)}) copy-start(f32[384]{0:T(512)S(1)} %get-tuple-element.114) | copy-start | bytes 4612
  38.1 164.7 %reduce-scatter.19.cloned.1.call-start = ((), (), s32[]{:S(2)}) async-start(), calls=%async_computation.17 | async-start | bytes 1966080 | tf_op jit(solution)/shard_map/reduce_scatter | solution.py:26
  75.8 4.6 slice-start.4
  93.4 48.5 %copy-start.62 = (s32[1,1024]{1,0:T(1,128)S(1)}, s32[1,1024]{1,0:T(1,128)}, u32[]{:S(2)}) copy-start(s32[1,1024]{1,0:T(1,128)} %param.20) | copy-start | bytes 12292
  143.8 6.8 copy-start.29
  146.2 4.4 copy-start.17
  153.2 4.7 copy-start.42
  154.9 4.7 copy-start.56
  154.9 30.9 %copy-start.51 = (bf16[384,192]{0,1:T(8,128)(2,1)S(1)}, bf16[384,192]{0,1:T(8,128)(2,1)}, u32[]{:S(2)}) copy-start(bf16[384,192]{0,1:T(8,128)(2,1)} %param.30) | copy-start | bytes 442372
  157.9 28.8 %copy-start.49 = (bf16[384,192]{0,1:T(8,128)(2,1)S(1)}, bf16[384,192]{0,1:T(8,128)(2,1)}, u32[]{:S(2)}) copy-start(bf16[384,192]{0,1:T(8,128)(2,1)} %param.29) | copy-start | bytes 442372
  159.5 68.7 %reduce-scatter.21.cloned.1.call-start = ((), (), s32[]{:S(2)}) async-start(), calls=%async_computation.18 | async-start | bytes 2359296 | tf_op jit(solution)/shard_map/reduce_scatter | solution.py:22
  186.7 16.2 %copy-start.15 = (bf16[1,256,384]{2,1,0:T(8,128)(2,1)S(1)}, bf16[1,256,384]{2,1,0:T(8,128)(2,1)}, u32[]{:S(2)}) copy-start(bf16[1,256,384]{2,1,0:T(8,128)(2,1)} %param.18) | copy-start | bytes 589828
  187.1 39.6 %copy-start.40 = (bf16[384,192]{0,1:T(8,128)(2,1)S(1)}, bf16[384,192]{0,1:T(8,128)(2,1)}, u32[]{:S(2)}) copy-start(bf16[384,192]{0,1:T(8,128)(2,1)} %param.28) | copy-start | bytes 442372
  188.5 47.8 %reduce-scatter.23.cloned.1.call-start = ((), (), s32[]{:S(2)}) async-start(), calls=%async_computation.19 | async-start | bytes 1179648 | tf_op jit(solution)/shard_map/reduce_scatter | solution.py:22
  228.1 63.8 %reduce-scatter.25.cloned.1.call-start = ((), (), s32[]{:S(2)}) async-start(), calls=%async_computation.20 | async-start | bytes 1966080 | tf_op jit(solution)/shard_map/reduce_scatter | solution.py:26
  241.1 4.7 copy-start.39
  242.8 4.7 copy-start.33
  242.8 33.6 %copy-start.37 = (bf16[512,384]{1,0:T(8,128)(2,1)S(1)}, bf16[512,384]{1,0:T(8,128)(2,1)}, u32[]{:S(2)}) copy-start(bf16[512,384]{1,0:T(8,128)(2,1)} %param.34) | copy-start | bytes 1179652
  247.4 72.2 %reduce-scatter.31.cloned.1.call-start = ((), (), s32[]{:S(2)}) async-start(), calls=%async_computation.24 | async-start | bytes 3145728 | tf_op jit(solution)/shard_map/reduce_scatter | solution.py:22
  278.5 37.0 %copy-start.36 = (bf16[384,512]{1,0:T(8,128)(2,1)S(1)}, bf16[384,512]{1,0:T(8,128)(2,1)}, u32[]{:S(2)}) copy-start(bf16[384,512]{1,0:T(8,128)(2,1)} %param.33) | copy-start | bytes 1179652
  278.5 53.0 %reduce-scatter.27.cloned.1.call-start = ((), (), s32[]{:S(2)}) async-start(), calls=%async_computation.21 | async-start | bytes 6291456 | tf_op jit(solution)/shard_map/reduce_scatter | solution.py:22
  319.6 28.5 %all-gather.13.cloned.1.call-start = ((), (), s32[]{:S(2)}) async-start(), calls=%async_computation.25 | async-start | bytes 3145728 | tf_op jit(solution)/shard_map/all_gather | solution.py:18
  336.1 52.6 %reduce-scatter.33.cloned.1.call-start = ((), (), s32[]{:S(2)}) async-start(), calls=%async_computation.26 | async-start | bytes 1966080 | tf_op jit(solution)/shard_map/reduce_scatter | solution.py:26
  352.1 69.5 %reduce-scatter.35.cloned.1.call-start = ((), (), s32[]{:S(2)}) async-start(), calls=%async_computation.27 | async-start | bytes 1179648 | tf_op jit(solution)/shard_map/reduce_scatter | solution.py:22
  413.7 22.4 %all-gather.11.cloned.1.call-start = ((), (), s32[]{:S(2)}) async-start(), calls=%async_computation.22 | async-start | bytes 1572864 | tf_op jit(solution)/shard_map/all_gather | solution.py:18
  414.5 58.4 %reduce-scatter.37.cloned.1.call-start = ((), (), s32[]{:S(2)}) async-start(), calls=%async_computation.28 | async-start | bytes 1966080 | tf_op jit(solution)/shard_map/reduce_scatter | solution.py:26
  422.6 4.0 copy-start.34
  422.6 4.1 slice-start.2
  422.6 4.8 slice-start.3
  433.9 5.3 copy-start.23
  435.6 73.9 %copy-start.24 = (f32[1,1,256,384]{3,2,1,0:T(8,128)S(1)}, f32[1,1,256,384]{3,2,1,0:T(8,128)}, u32[]{:S(2)}) copy-start(f32[1,1,256,384]{3,2,1,0:T(8,128)} %reduce-scatter.33.cloned.1.call-done) | copy-start | bytes 1179652
  435.6 73.8 %reduce-scatter.29.cloned.1.call-start = ((), (), s32[]{:S(2)}) async-start(), calls=%async_computation.23 | async-start | bytes 1966080 | tf_op jit(solution)/shard_map/reduce_scatter | solution.py:26
  439.2 91.5 %copy-start.43 = (bf16[192,384]{1,0:T(8,128)(2,1)S(1)}, bf16[192,384]{1,0:T(8,128)(2,1)}, u32[]{:S(2)}) copy-start(bf16[192,384]{1,0:T(8,128)(2,1)} %param.27) | copy-start | bytes 442372
  439.2 100.5 %reduce-scatter.39.cloned.1.call-start = ((), (), s32[]{:S(2)}) async-start(), calls=%async_computation.29 | async-start | bytes 1179648 | tf_op jit(solution)/shard_map/reduce_scatter | solution.py:22
  532.0 38.4 %reduce-scatter.41.cloned.1.call-start = ((), (), s32[]{:S(2)}) async-start(), calls=%async_computation.30 | async-start | bytes 2359296 | tf_op jit(solution)/shard_map/reduce_scatter | solution.py:22
  540.7 8.0 %slice-start = ((s8[6291456]{0:T(1024)(128)(4,1)}), s8[4194304]{0:T(1024)(128)(4,1)S(1)}, s32[]{:S(2)}) async-start(s8[6291456]{0:T(1024)(128)(4,1)} %bitcast.277), calls=%async_computation.36 | async-start | bytes 8388608
  552.2 23.7 %reduce-scatter.45.cloned.1.call-start = ((), (), s32[]{:S(2)}) async-start(), calls=%async_computation.33 | async-start | bytes 2359296 | tf_op jit(solution)/shard_map/reduce_scatter | solution.py:22
  560.1 26.8 %all-gather.15.cloned.1.call-start = ((), (), s32[]{:S(2)}) async-start(), calls=%async_computation.31 | async-start | bytes 1769472 | tf_op jit(solution)/shard_map/all_gather | solution.py:18
  560.1 6.1 copy-start.10
  560.1 6.1 copy-start.28
  563.3 4.3 copy-start.12
  563.3 4.3 copy-start.22
  573.4 9.6 %copy-start.20 = (bf16[1,1,1024,192]{2,3,1,0:T(8,128)(2,1)S(1)}, bf16[1,1,1024,192]{2,3,1,0:T(8,128)(2,1)}, u32[]{:S(2)}) copy-start(bf16[1,1,1024,192]{2,3,1,0:T(8,128)(2,1)} %copy-done.19) | copy-start | bytes 1179652
  573.4 128.0 %all-reduce.8.cloned.1.call-start = ((), (), s32[]{:S(2)}) async-start(), calls=%async_computation.35 | async-start | bytes 4718592 | tf_op jit(solution)/shard_map/psum | solution.py:360
  575.8 6.1 copy-start.7
  575.8 7.2 copy-start.14
  584.1 9.8 %copy-start.44 = (bf16[384,192]{0,1:T(8,128)(2,1)S(1)}, bf16[384,192]{0,1:T(8,128)(2,1)}, u32[]{:S(2)}) copy-start(bf16[384,192]{0,1:T(8,128)(2,1)} %param.25) | copy-start | bytes 442372
  593.8 123.0 %reduce-scatter.43.cloned.1.call-start = ((), (), s32[]{:S(2)}) async-start(), calls=%async_computation.32 | async-start | bytes 1966080 | tf_op jit(solution)/shard_map/reduce_scatter | solution.py:26
  599.6 165.1 %reduce-scatter.47.cloned.1.call-start = ((), (), s32[]{:S(2)}) async-start(), calls=%async_computation.34 | async-start | bytes 1966080 | tf_op jit(solution)/shard_map/reduce_scatter | solution.py:26
  695.3 5.5 copy-start.64
  701.4 11.8 %copy-start.57 = (bf16[192,384]{1,0:T(8,128)(2,1)S(1)}, bf16[192,384]{1,0:T(8,128)(2,1)}, u32[]{:S(2)}) copy-start(bf16[192,384]{1,0:T(8,128)(2,1)} %get-tuple-element.139) | copy-start | bytes 442372
  701.4 12.5 %copy-start.55 = (bf16[384,512]{1,0:T(8,128)(2,1)S(1)}, bf16[384,512]{1,0:T(8,128)(2,1)}, u32[]{:S(2)}) copy-start(bf16[384,512]{1,0:T(8,128)(2,1)} %get-tuple-element.140) | copy-start | bytes 1179652
  701.4 13.5 %copy-start.54 = (bf16[384,512]{1,0:T(8,128)(2,1)S(1)}, bf16[384,512]{1,0:T(8,128)(2,1)}, u32[]{:S(2)}) copy-start(bf16[384,512]{1,0:T(8,128)(2,1)} %get-tuple-element.141) | copy-start | bytes 1179652
  701.4 14.5 %copy-start.53 = (bf16[512,384]{1,0:T(8,128)(2,1)S(1)}, bf16[512,384]{1,0:T(8,128)(2,1)}, u32[]{:S(2)}) copy-start(bf16[512,384]{1,0:T(8,128)(2,1)} %get-tuple-element.142) | copy-start | bytes 1179652
  704.8 12.0 %copy-start.16 = (bf16[1,256,384]{2,1,0:T(8,128)(2,1)S(1)}, bf16[1,256,384]{2,1,0:T(8,128)(2,1)}, u32[]{:S(2)}) copy-start(bf16[1,256,384]{2,1,0:T(8,128)(2,1)} %param.18) | copy-start | bytes 589828
  704.8 12.0 %copy-start.59 = (f32[384]{0:T(512)S(1)}, f32[384]{0:T(512)}, u32[]{:S(2)}) copy-start(f32[384]{0:T(512)} %copy-done.58) | copy-start | bytes 4612
  704.8 12.0 %copy-start.61 = (f32[1,256]{1,0:T(1,128)S(1)}, f32[1,256]{1,0:T(1,128)}, u32[]{:S(2)}) copy-start(f32[1,256]{1,0:T(1,128)} %copy-done.60) | copy-start | bytes 3076
  706.5 56.2 %copy-start.38 = (f32[1,256,384]{2,1,0:T(8,128)S(1)}, f32[1,256,384]{2,1,0:T(8,128)}, u32[]{:S(2)}) copy-start(f32[1,256,384]{2,1,0:T(8,128)} %get-tuple-element.144) | copy-start | bytes 1179652
  711.5 53.2 %copy-start.1 = (bf16[384,512]{1,0:T(8,128)(2,1)S(1)}, bf16[384,512]{1,0:T(8,128)(2,1)}, u32[]{:S(2)}) copy-start(bf16[384,512]{1,0:T(8,128)(2,1)} %param.32) | copy-start | bytes 1179652
  (26 other events, 50.7 us)
Sparse Core Ops, SparseCore 0:
  38.3 9.6 reduce-scatter.16
  159.6 43.2 reduce-scatter.18
  205.2 9.7 reduce-scatter.20
  228.2 7.9 reduce-scatter.22
  247.6 44.2 reduce-scatter.24
  294.1 10.9 reduce-scatter.30
  319.7 11.7 reduce-scatter.26
  336.2 11.8 all-gather.12
  352.2 36.4 reduce-scatter.32
  413.8 7.7 reduce-scatter.34
  423.7 10.4 all-gather.10
  436.4 36.4 reduce-scatter.36
  475.2 34.2 reduce-scatter.28
  532.1 7.5 reduce-scatter.38
  552.3 10.2 reduce-scatter.40
  564.7 10.2 reduce-scatter.44
  576.4 10.4 all-gather.14
  593.9 77.4 all-reduce.7
  673.7 35.2 reduce-scatter.42
  711.8 34.6 reduce-scatter.46
where the time goes:
time: 787 us; the launch traced here: 772 us
  blocking collectives  222 us (28%)
  local copies, waits for them, and re-layouts  207 us (26%)
  waiting for transfers between devices  177 us (22%)
  matrix products  86.9 us (11%)
  other arithmetic  61.9 us (8%)
  between operations  15.5 us (2%)
    all_gather x7, blocking collectives, rows_over_x(): return lax.all_gather(stacked, 'gx', axis=2, tiled=True)  151 us
    reduce_scatter x7, waiting for transfers between devices, sums_over_x(): return lax.psum_scatter(stacked, 'gx', scatter_dimension=2, tiled=True)  131 us
    unnamed x145, local copies, waits for them, and re-layouts  71.9 us
    rev x1, local copies, waits for them, and re-layouts, distance_grid(): return matrix[:, ::-1, :]  48.5 us
    psum x1, blocking collectives, body(): grad_gains, grad_rel = lax.psum((gain_full, rel_full), ('dp', 'gx', 'gy'))  42.2 us
    rev x1, local copies, waits for them, and re-layouts, diagonal_sums(): flipped = matrix[:, ::-1, :]  31.7 us
    reduce_scatter x9, waiting for transfers between devices, sums_over_y(): return lax.psum_scatter(stacked, 'gy', scatter_dimension=2, tiled=True)  30.9 us
    dot_general x11, matrix products, weight_grad(): jnp.einsum('tkv,tkb->vb', collected_shards, gradient_row_block, preferred...  22.2 us
  transfers between devices with their start and end apart: 20, of which 11 were waited for; matrix products, arithmetic and copies ran while one was open for 36% of the time, Pallas kernels for 0%

commit v1 on v0

v1 whole, which is shorter than its diff:
```python
import functools

import jax
import jax.numpy as jnp
from jax import lax
from jax.experimental import pallas as pl
from jax.experimental.pallas import tpu as pltpu
from jax.sharding import PartitionSpec as P

DH = 64
epsilon = 1e-06
masked_score = -1000000000.0
f32 = jnp.float32
bf16 = jnp.bfloat16
VMEM_LIMIT = 48 * 1024 * 1024


def mm(a, b):
    return jnp.dot(a, b, preferred_element_type=f32)


def mm_t(a, b):
    return lax.dot_general(a, b, (((1,), (1,)), ((), ())), preferred_element_type=f32)


def t_mm(a, b):
    return lax.dot_general(a, b, (((0,), (0,)), ((), ())), preferred_element_type=f32)


def gather_tokens(own):
    return lax.all_gather(own, "gx", axis=0, tiled=True)


def scatter_tokens(partial_sums):
    return lax.psum_scatter(
        partial_sums.astype(bf16), "gx", scatter_dimension=0, tiled=True
    ).astype(f32)


def swap(value):
    size = lax.axis_size("gy")
    return lax.ppermute(value, "gy", [(i, size - 1 - i) for i in range(size)])


def natural_rows(pair_ref, width, start, block):
    pieces = []
    for b in range(2 * (width // (2 * block))):
        pieces.append(pair_ref[b % 2, (b // 2) * block : (b // 2 + 1) * block, start : start + DH])
    return jnp.concatenate(pieces, axis=0)


def softmax_rows(scores):
    top = jnp.max(scores, axis=-1, keepdims=True)
    e = jnp.exp(scores - top)
    return e * (1.0 / jnp.sum(e, axis=-1, keepdims=True))


def bias_tile(vec_ref, head, block):
    row = vec_ref[head : head + 1, :]
    return pltpu.roll(
        jnp.broadcast_to(row, (block, row.shape[1])), 0, 1, stride=1, stride_axis=0
    )


def rotate_lanes(x, amount):
    if amount == 0:
        return x
    width = x.shape[1]
    return jnp.concatenate([x[:, width - amount :], x[:, : width - amount]], axis=1)


def self_mask(core_ref, dq_ref, dk_ref, g, width, block):
    first = (2 * g + core_ref[0]) * block
    rows = first + lax.broadcasted_iota(jnp.int32, (block, width), 0)
    cols = lax.broadcasted_iota(jnp.int32, (block, width), 1)
    own = dq_ref[g * block : (g + 1) * block, :]
    return (cols <= rows) & (own == dk_ref[:, :width])


def self_scores(q, k, tile, mask, g, width, block):
    return jnp.where(mask, mm_t(q, k) + rotate_lanes(tile, 2 * block * g)[:, :width], masked_score)


def self_forward_kernel(block, heads, core_ref, q_ref, kv_ref, dq_ref, dk_ref, vec_ref, out_ref):
    groups = q_ref.shape[0] // block
    keys = 2 * q_ref.shape[0]
    masks = [
        self_mask(core_ref, dq_ref, dk_ref, g, 2 * block * (g + 1), block) for g in range(groups)
    ]
    parts = [[] for _ in range(groups)]
    for h in range(heads):
        k = natural_rows(kv_ref, keys, h * DH, block)
        v = natural_rows(kv_ref, keys, (heads + h) * DH, block)
        tile = bias_tile(vec_ref, h, block)
        for g in range(groups):
            width = 2 * block * (g + 1)
            q = q_ref[g * block : (g + 1) * block, h * DH : (h + 1) * DH]
            p = softmax_rows(self_scores(q, k[:width], tile, masks[g], g, width, block))
            parts[g].append(mm(p.astype(bf16), v[:width]))
    for g in range(groups):
        out_ref[g * block : (g + 1) * block, :] = jnp.concatenate(parts[g], axis=1).astype(bf16)


def self_backward_kernel(
    block, heads, core_ref, q_ref, kv_ref, dq_ref, dk_ref, vec_ref, dc_ref, gq_ref, gkv_ref, gd_ref
):
    groups = q_ref.shape[0] // block
    keys = 2 * q_ref.shape[0]
    masks = [
        self_mask(core_ref, dq_ref, dk_ref, g, 2 * block * (g + 1), block) for g in range(groups)
    ]
    flip = (
        lax.broadcasted_iota(jnp.int32, (block, block), 0)
        + lax.broadcasted_iota(jnp.int32, (block, block), 1)
        == block - 1
    ).astype(bf16)
    parts = [[] for _ in range(groups)]
    gd_ref[...] = jnp.zeros_like(gd_ref)
    for h in range(heads):
        k = natural_rows(kv_ref, keys, h * DH, block)
        v = natural_rows(kv_ref, keys, (heads + h) * DH, block)
        tile = bias_tile(vec_ref, h, block)
        gk_total = None
        gv_total = None
        shifted = None
        for g in range(groups - 1, -1, -1):
            width = 2 * block * (g + 1)
            q = q_ref[g * block : (g + 1) * block, h * DH : (h + 1) * DH]
            dc = dc_ref[g * block : (g + 1) * block, h * DH : (h + 1) * DH]
            p = softmax_rows(self_scores(q, k[:width], tile, masks[g], g, width, block))
            dp = mm_t(dc, v[:width])
            inner = jnp.sum(dp * p, axis=-1, keepdims=True)
            ds = (p * (dp - inner)).astype(bf16)
            parts[g].append(mm(ds, k[:width]))
            gk = t_mm(q, ds)
            gv = t_mm(dc, p.astype(bf16))
            flipped = mm(flip, ds)
            if gk_total is None:
                gk_total, gv_total = gk, gv
                shifted = rotate_lanes(flipped, keys - 2 * block * g) if g else flipped
            else:
                rest = jnp.zeros((DH, keys - width), f32)
                gk_total = gk_total + jnp.concatenate([gk, rest], axis=1)
                gv_total = gv_total + jnp.concatenate([gv, rest], axis=1)
                flipped = jnp.concatenate(
                    [flipped, jnp.zeros((block, keys - width), f32)], axis=1
                )
                if g:
                    flipped = rotate_lanes(flipped, keys - 2 * block * g)
                shifted = shifted + flipped
        for b in range(2 * groups):
            lanes = slice((b // 2) * block, (b // 2 + 1) * block)
            source = slice(b * block, (b + 1) * block)
            gkv_ref[b % 2, h * DH : (h + 1) * DH, lanes] = gk_total[:, source].astype(bf16)
            gkv_ref[b % 2, (heads + h) * DH : (heads + h + 1) * DH, lanes] = gv_total[
                :, source
            ].astype(bf16)
        gd_ref[h : h + 1, :] = jnp.sum(
            pltpu.roll(shifted, 0, 1, stride=1, stride_axis=0), axis=0, keepdims=True
        )
    for g in range(groups):
        gq_ref[g * block : (g + 1) * block, :] = jnp.concatenate(parts[g], axis=1).astype(bf16)


def cross_forward_kernel(block, heads, q_ref, kv_ref, out_ref):
    rows = q_ref.shape[0]
    for h in range(heads):
        k = jnp.concatenate([kv_ref[c, :, h * DH : (h + 1) * DH] for c in range(2)], axis=0)
        v = jnp.concatenate(
            [kv_ref[c, :, (heads + h) * DH : (heads + h + 1) * DH] for c in range(2)], axis=0
        )
        for r in range(0, rows, block):
            p = softmax_rows(mm_t(q_ref[r : r + block, h * DH : (h + 1) * DH], k))
            out_ref[r : r + block, h * DH : (h + 1) * DH] = mm(p.astype(bf16), v).astype(bf16)


def cross_backward_kernel(block, heads, q_ref, kv_ref, dc_ref, gq_ref, gkv_ref):
    rows = q_ref.shape[0]
    for h in range(heads):
        k = jnp.concatenate([kv_ref[c, :, h * DH : (h + 1) * DH] for c in range(2)], axis=0)
        v = jnp.concatenate(
            [kv_ref[c, :, (heads + h) * DH : (heads + h + 1) * DH] for c in range(2)], axis=0
        )
        gk_total = None
        for r in range(0, rows, block):
            q = q_ref[r : r + block, h * DH : (h + 1) * DH]
            dc = dc_ref[r : r + block, h * DH : (h + 1) * DH]
            p = softmax_rows(mm_t(q, k))
            dp = mm_t(dc, v)
            inner = jnp.sum(dp * p, axis=-1, keepdims=True)
            ds = (p * (dp - inner)).astype(bf16)
            gq_ref[r : r + block, h * DH : (h + 1) * DH] = mm(ds, k).astype(bf16)
            gk = t_mm(q, ds)
            gv = t_mm(dc, p.astype(bf16))
            gk_total = gk if gk_total is None else gk_total + gk
            gv_total = gv if r == 0 else gv_total + gv
        for c in range(2):
            source = slice(c * rows, (c + 1) * rows)
            gkv_ref[c, h * DH : (h + 1) * DH, :] = gk_total[:, source].astype(bf16)
            gkv_ref[c, (heads + h) * DH : (heads + h + 1) * DH, :] = gv_total[:, source].astype(
                bf16
            )


def call(kernel, out_shape, smem, name):
    vm = pl.BlockSpec(memory_space=pltpu.VMEM)

    def run(*operands):
        specs = [pl.BlockSpec(memory_space=pltpu.SMEM)] * smem + [vm] * (len(operands) - smem)
        multi = isinstance(out_shape, (list, tuple))
        return pl.pallas_call(
            kernel,
            out_shape=out_shape,
            in_specs=specs,
            out_specs=[vm] * len(out_shape) if multi else vm,
            compiler_params=pltpu.CompilerParams(vmem_limit_bytes=VMEM_LIMIT),
            name=name,
        )(*operands)

    return run


def norm_forward(stream, gain):
    root = lax.rsqrt(jnp.mean(stream * stream, axis=-1, keepdims=True) + epsilon)
    plain = stream * root
    return (plain * gain).astype(bf16), plain, root


def norm_backward(dy, plain, root, gain):
    scaled = dy * gain
    inner = jnp.mean(scaled * plain, axis=-1, keepdims=True)
    return root * (scaled - plain * inner), jnp.sum(dy * plain, axis=0)


def glu_piece(gate, up_part):
    return jax.nn.gelu(gate, approximate=True) * up_part


def body(
    hidden_in,
    encoded,
    doc_ids,
    buckets,
    rel_table,
    norm_gains,
    self_q,
    self_k,
    self_v,
    self_out,
    cross_q,
    cross_k,
    cross_v,
    cross_out,
    ff_gate,
    ff_up,
    ff_down,
    grad_out,
):
    core = lax.axis_index("gy")
    column = lax.axis_index("gx")
    groups = lax.axis_size("gx")
    seq_len = doc_ids.shape[1]
    half = hidden_in.shape[2]
    block = hidden_in.shape[1] // 2
    proj = self_q.shape[1]
    heads = proj // DH
    hid_part = ff_gate.shape[1]
    own_tokens = groups * block
    core_one = core.reshape(1).astype(jnp.int32)

    def to_rows(x):
        return lax.all_to_all(x, "gy", x.ndim - 2, x.ndim - 1, tiled=True)

    def to_features(x):
        return lax.all_to_all(x, "gy", x.ndim - 1, x.ndim - 2, tiled=True)

    first_rows = to_rows(hidden_in[0])
    w_self = lax.all_gather(
        jnp.concatenate([self_q, self_k, self_v], axis=1), "gy", axis=0, tiled=True
    )
    both_rows = to_rows(jnp.concatenate([encoded, grad_out], axis=0))
    w_cross = lax.all_gather(
        jnp.concatenate([cross_q, cross_k, cross_v], axis=1), "gy", axis=0, tiled=True
    )
    w_ff = lax.all_gather(jnp.concatenate([ff_gate, ff_up], axis=1), "gy", axis=0, tiled=True)
    w_outs = lax.all_gather(
        jnp.concatenate([self_out, cross_out, ff_down], axis=0), "gy", axis=1, tiled=True
    )
    w_self_out, w_cross_out, w_down = (
        w_outs[:proj],
        w_outs[proj : 2 * proj],
        w_outs[2 * proj :],
    )
    w_cq, w_ckv = w_cross[:, :proj], w_cross[:, proj:]

    distance_from = (core * block - jnp.arange(seq_len, dtype=jnp.int32)) % seq_len
    table_part = lax.dynamic_slice_in_dim(rel_table, column * heads, heads, 1)

    def hot(distances):
        return (
            buckets[distances][None, :]
            == jnp.arange(rel_table.shape[0], dtype=jnp.int32)[:, None]
        ).astype(f32)

    bias_vec = lax.dot_general(
        table_part,
        hot(distance_from),
        (((0,), (0,)), ((), ())),
        precision=lax.Precision.HIGHEST,
    )
    docs_k = doc_ids
    docs_q = lax.dynamic_index_in_dim(
        doc_ids.reshape(groups, 2, block), core, 1, keepdims=False
    ).reshape(own_tokens, 1)

    stream0 = first_rows.astype(f32)
    low_one, plain_one, root_one = norm_forward(stream0, norm_gains[0])
    rows_one = gather_tokens(low_one)
    qkv = mm(rows_one, w_self).astype(bf16)
    q1 = qkv[:, :proj]
    kv1 = lax.all_gather(qkv[:, proj:], "gy", axis=0)

    enc_rows = gather_tokens(both_rows[0])
    kv2_own = mm(enc_rows, w_ckv).astype(bf16)
    kv2 = lax.all_gather(kv2_own, "gy", axis=0)
    out_rows = gather_tokens(both_rows[1])
    d_hid = mm_t(out_rows, w_down)

    ctx1 = call(
        functools.partial(self_forward_kernel, block, heads),
        jax.ShapeDtypeStruct((own_tokens, proj), bf16),
        1,
        "self_forward",
    )(core_one, q1, kv1, docs_q, docs_k, bias_vec)
    stream1 = stream0 + scatter_tokens(mm(ctx1, w_self_out))
    low_two, plain_two, root_two = norm_forward(stream1, norm_gains[1])
    rows_two = gather_tokens(low_two)
    q2 = mm(rows_two, w_cq).astype(bf16)
    ctx2 = call(
        functools.partial(cross_forward_kernel, 2 * block, heads),
        jax.ShapeDtypeStruct((own_tokens, proj), bf16),
        0,
        "cross_forward",
    )(q2, kv2)
    stream2 = stream1 + scatter_tokens(mm(ctx2, w_cross_out))
    low_three, plain_three, root_three = norm_forward(stream2, norm_gains[2])
    rows_three = gather_tokens(low_three)
    gate_up = mm(rows_three, w_ff)
    hidden_float, glu_pull = jax.vjp(glu_piece, gate_up[:, :hid_part], gate_up[:, hid_part:])
    hid = hidden_float.astype(bf16)
    d_gate, d_up = glu_pull(d_hid)
    d_gu = jnp.concatenate([d_gate, d_up], axis=1).astype(bf16)

    def own_half(x, which):
        return lax.dynamic_slice_in_dim(x, which * half, half, 1)

    def grad_cols(rows, d):
        other = t_mm(own_half(rows, 1 - core), d).astype(bf16)
        return t_mm(own_half(rows, core), d) + swap(other).astype(f32)

    def grad_rows(left, rows):
        other = t_mm(left, own_half(rows, 1 - core)).astype(bf16)
        return t_mm(left, own_half(rows, core)) + swap(other).astype(f32)

    def over_sequences(value):
        return lax.psum(value.astype(bf16), "dp")

    back_partial = mm_t(d_gu, w_ff)
    dn3 = scatter_tokens(back_partial)
    layer_rows = (stream2 + scatter_tokens(mm(hid, w_down))).astype(bf16)
    layer_out = to_features(layer_rows)[None]
    g_gu = grad_cols(rows_three, d_gu)
    g_down = grad_rows(hid, out_rows)
    back_three, gain_three = norm_backward(dn3, plain_three, root_three, norm_gains[2])
    g2 = both_rows[1].astype(f32) + back_three
    rows_a2 = gather_tokens(g2.astype(bf16))
    dctx2 = mm_t(rows_a2, w_cross_out).astype(bf16)
    dq2, dkv2_both = call(
        functools.partial(cross_backward_kernel, 2 * block, heads),
        (
            jax.ShapeDtypeStruct((own_tokens, proj), bf16),
            jax.ShapeDtypeStruct((2, 2 * proj, own_tokens), bf16),
        ),
        0,
        "cross_backward",
    )(q2, kv2, dctx2)

    def pair_sum(both):
        other = lax.dynamic_index_in_dim(both, 1 - core, 0, keepdims=False)
        own = lax.dynamic_index_in_dim(both, core, 0, keepdims=False)
        return (own.astype(f32) + swap(other).astype(f32)).astype(bf16)

    dn2 = scatter_tokens(mm_t(dq2, w_cq))
    dkv2 = pair_sum(dkv2_both)
    back_two, gain_two = norm_backward(dn2, plain_two, root_two, norm_gains[1])
    g1 = g2 + back_two
    rows_a1 = gather_tokens(g1.astype(bf16))
    dctx1 = mm_t(rows_a1, w_self_out).astype(bf16)
    grad_encoded = to_features(
        scatter_tokens(lax.dot_general(dkv2, w_ckv, (((0,), (1,)), ((), ())), preferred_element_type=f32))
    )[None]
    g_cq = grad_cols(rows_two, dq2)

    def grad_cols_t(rows, d_t):
        other = mm(d_t, own_half(rows, 1 - core)).astype(bf16)
        return (mm(d_t, own_half(rows, core)) + swap(other).astype(f32)).T

    g_ckv = grad_cols_t(enc_rows, dkv2)
    g_cross_out = grad_rows(ctx2, rows_a2)

    dq1, dkv1_both, by_shift = call(
        functools.partial(self_backward_kernel, block, heads),
        (
            jax.ShapeDtypeStruct((own_tokens, proj), bf16),
            jax.ShapeDtypeStruct((2, 2 * proj, own_tokens), bf16),
            jax.ShapeDtypeStruct((8, seq_len), f32),
        ),
        1,
        "self_backward",
    )(core_one, q1, kv1, docs_q, docs_k, bias_vec, dctx1)
    dkv1 = pair_sum(dkv1_both)
    dn1 = scatter_tokens(
        mm_t(dq1, w_self[:, :proj])
        + lax.dot_general(dkv1, w_self[:, proj:], (((0,), (1,)), ((), ())), preferred_element_type=f32)
    )
    back_one, gain_one = norm_backward(dn1, plain_one, root_one, norm_gains[0])
    grad_hidden = to_features(g1 + back_one)[None]
    g_q = grad_cols(rows_one, dq1)
    g_kv = grad_cols_t(rows_one, dkv1)
    g_self_out = grad_rows(ctx1, rows_a1)

    shift_distance = (
        core * block + block - 1 - jnp.arange(seq_len, dtype=jnp.int32)
    ) % seq_len
    table_grad = lax.dot_general(
        hot(shift_distance),
        by_shift[:heads],
        (((1,), (1,)), ((), ())),
        precision=lax.Precision.HIGHEST,
    )
    rel_full = lax.dynamic_update_slice(
        jnp.zeros(rel_table.shape, f32), table_grad, (0, column * heads)
    )
    gains = jnp.stack([gain_one, gain_two, gain_three])
    grad_gains, grad_rel = lax.psum((gains, rel_full), ("dp", "gx", "gy"))

    ff_flat = jnp.concatenate([g_gu.reshape(-1), g_down.reshape(-1)])
    ff_sum = over_sequences(ff_flat).astype(f32)
    cut = g_gu.size
    s_gu = ff_sum[:cut].reshape(g_gu.shape)
    s_down = ff_sum[cut:].reshape(g_down.shape)
    s_cross = over_sequences(jnp.concatenate([g_cq, g_ckv], axis=1)).astype(f32)
    s_cross_out = over_sequences(g_cross_out).astype(f32)
    s_self = over_sequences(jnp.concatenate([g_q, g_kv], axis=1)).astype(f32)
    s_self_out = over_sequences(g_self_out).astype(f32)
    return (
        layer_out,
        grad_hidden,
        grad_encoded,
        grad_gains,
        grad_rel,
        s_self[:, :proj],
        s_self[:, proj : 2 * proj],
        s_self[:, 2 * proj :],
        s_self_out,
        s_cross[:, :proj],
        s_cross[:, proj : 2 * proj],
        s_cross[:, 2 * proj :],
        s_cross_out,
        s_gu[:, :hid_part],
        s_gu[:, hid_part:],
        s_down,
    )


def solution(mesh):
    placed = (
        P("dp", "gx", "gy"),
        P("dp", "gx", "gy"),
        P("dp", None),
        P(),
        P(),
        P(),
        P("gy", "gx"),
        P("gy", "gx"),
        P("gy", "gx"),
        P("gx", "gy"),
        P("gy", "gx"),
        P("gy", "gx"),
        P("gy", "gx"),
        P("gx", "gy"),
        P("gy", "gx"),
        P("gy", "gx"),
        P("gx", "gy"),
        P("dp", "gx", "gy"),
    )
    return jax.shard_map(
        body,
        mesh=mesh,
        in_specs=placed,
        out_specs=(
            P("dp", "gx", "gy"),
            P("dp", "gx", "gy"),
            P("dp", "gx", "gy"),
            P(),
            P(),
            P("gy", "gx"),
            P("gy", "gx"),
            P("gy", "gx"),
            P("gx", "gy"),
            P("gy", "gx"),
            P("gy", "gx"),
            P("gy", "gx"),
            P("gx", "gy"),
            P("gy", "gx"),
            P("gy", "gx"),
            P("gx", "gy"),
        ),
        check_vma=False,
    )
```

time: 787 us -> 455 us (0.58)
  local copies, waits for them, and re-layouts: 207 us -> 30.2 us
  waiting for transfers between devices: 177 us -> 86.1 us
  matrix products: 86.9 us -> 42.4 us
  other arithmetic: 61.9 us -> 22.2 us
  Pallas kernels: 0 us -> 22.6 us
    reduce_scatter x16 -> x7, waiting for transfers between devices: 162 us -> 52.6 us  [scatter_tokens(): lax.psum_scatter(partial_sums.astype(bf16), 'gx', scatter_dimension=0, ti...]
    rev x3 -> x0, local copies, waits for them, and re-layouts: 81.6 us -> none  [the longest x1 48.5 us: distance_grid(): return matrix[:, ::-1, :]]
    unnamed x145 -> x118, local copies, waits for them, and re-layouts: 71.9 us -> 8.85 us
    dot_general x47 -> x33, matrix products: 86.9 us -> 42.4 us  [the longest x11 16.8 us: mm(): return jnp.dot(a, b, preferred_element_type=f32)]
    psum x1, waiting for transfers between devices: 0.02 us -> 33 us  [over_sequences(): return lax.psum(value.astype(bf16), 'dp')]
    convert_element_type x25 -> x9, other arithmetic: 30.7 us -> 6.14 us  [the longest x1 1.97 us: body(): rows_a1 = gather_tokens(g1.astype(bf16))]
    pallas_call x0 -> x4, Pallas kernels: none -> 22.6 us  [run(): pl.pallas_call(kernel, out_shape=out_shape, in_specs=specs, out_specs=[vm...]
    another operation x5 -> x3, local copies, waits for them, and re-layouts: 19.5 us -> 0.01 us  [body(): gains = jnp.stack([gain_one, gain_two, gain_three])]
  transfers between devices with their start and end apart: 20 -> 21, of which waited for: 11 -> 6; matrix products, arithmetic and copies ran while one was open for 36% -> 12% of each run, Pallas kernels for 0% -> 3%
where the time goes in v1:
time: 455 us; the launch traced here: 447 us
  blocking collectives  222 us (49%)
  waiting for transfers between devices  86.1 us (19%)
  matrix products  42.4 us (9%)
  local copies, waits for them, and re-layouts  30.2 us (7%)
  Pallas kernels  22.6 us (5%)
  other arithmetic  22.2 us (5%)
  between operations  15.6 us (3%)
  starting transfers between devices  6.61 us (1%)
    all_gather x7, blocking collectives, gather_tokens(): return lax.all_gather(own, 'gx', axis=0, tiled=True)  155 us
    reduce_scatter x7, waiting for transfers between devices, scatter_tokens(): lax.psum_scatter(partial_sums.astype(bf16), 'gx', scatter_dimension=0, ti...  52.6 us
    psum x1, blocking collectives, body(): grad_gains, grad_rel = lax.psum((gains, rel_full), ('dp', 'gx', 'gy'))  39.5 us
    psum x1, waiting for transfers between devices, over_sequences(): return lax.psum(value.astype(bf16), 'dp')  33 us
    pallas_call x4, Pallas kernels, run(): pl.pallas_call(kernel, out_shape=out_shape, in_specs=specs, out_specs=[vm...  22.6 us
    dot_general x11, matrix products, mm(): return jnp.dot(a, b, preferred_element_type=f32)  16.8 us
    all_to_all x3, blocking collectives, to_features(): return lax.all_to_all(x, 'gy', x.ndim - 1, x.ndim - 2, tiled=True)  13.6 us
    dot_general x12, matrix products, t_mm(): lax.dot_general(a, b, (((0,), (0,)), ((), ())), preferred_element_type=f32)  13.1 us
  transfers between devices with their start and end apart: 21, of which 6 were waited for; matrix products, arithmetic and copies ran while one was open for 12% of the time, Pallas kernels for 3%

profile of v1, /device:TPU:0, one launch (start us, length us, event | category | flops | bytes accessed | tf_op | source)
XLA Modules:
  0.0 447.3 jit_solution(2355304337026598889)
XLA Ops:
  7.2 3.4 all-to-all-start
  10.7 2.0 pad_maximum_fusion.3
  13.2 21.2 %all_gather.45 = bf16[512,768]{1,0:T(8,128)(2,1)S(1)} all-gather(bf16[128,768]{1,0:T(8,128)(2,1)S(1)} %multiply_convert_fusion.4), channel_id=1, replica_groups=mesh['dp'=4,'gx'=4,'gy'=2] {'gx'}, dimensions={0}, use_global_device_ids=true | all-gather | bytes 983040 | tf_op jit(solution)/shard_map/all_gather | solution.py:31
  34.6 2.4 all_gather.46
  38.5 4.5 %gather_fusion = s32[1024]{0:T(1024)S(1)} fusion(s32[1024]{0:T(1024)S(1)} %copy-done.5, s32[1024]{0:T(1024)S(1)} %broadcast_clamp_fusion.1), kind=kCustom, calls=%fused_computation | custom fusion | bytes 12288 | tf_op jit(solution)/shard_map/gather | solution.py:301
  43.1 2.4 all-gather
  45.6 5.3 %self_forward.1 = bf16[512,192]{1,0:T(8,128)(2,1)S(1)} custom-call(s32[1]{0:T(128)} %bitcast.2.core_ref, bf16[512,192]{1,0:T(8,128)(2,1)S(1)} %slice.140.q_ref, bf16[2,512,384]{2,1,0:T(8,128)(2,1)S(1)} %bitcast.94, s32[512,1]{1,0:T(8,128)S(1)} %copy.94.dq_ref, s32[1,1024]{1,0:T(1,128)S(1)} %copy-done.4, f32[3,1024]{1,0:T(4,128)S(1)} %fusion.73.vec_ref), custom_call_target="tpu_custom_call" | custom-call | tf_op jit(solution)/shard_map/self_forward/pallas_call | solution.py:211
  50.9 2.2 convolution_convert_fusion.5
  53.7 4.2 all_to_all.80
  58.7 2.4 all_gather.51
  61.1 26.6 %all_gather.52 = bf16[512,768]{1,0:T(8,128)(2,1)S(1)} all-gather(bf16[128,768]{1,0:T(8,128)(2,1)S(1)} %bitcast.120), channel_id=1, replica_groups=mesh['dp'=4,'gx'=4,'gy'=2] {'gx'}, dimensions={0}, use_global_device_ids=true | all-gather | bytes 983040 | tf_op jit(solution)/shard_map/all_gather | solution.py:31
  89.2 2.4 all-gather.1
  91.5 1.2 multiply_reduce_fusion.1
  92.9 17.8 %all_gather.50 = bf16[512,768]{1,0:T(8,128)(2,1)S(1)} all-gather(bf16[128,768]{1,0:T(8,128)(2,1)S(1)} %multiply_convert_fusion.3), channel_id=1, replica_groups=mesh['dp'=4,'gx'=4,'gy'=2] {'gx'}, dimensions={0}, use_global_device_ids=true | all-gather | bytes 983040 | tf_op jit(solution)/shard_map/all_gather | solution.py:31
  110.7 1.5 convolution_convert_fusion.12.q_ref
  112.3 3.8 cross_forward.1
  116.1 2.2 convolution_convert_fusion.4
  118.3 2.1 pad_maximum_fusion.2
  121.2 27.5 %all_gather.57 = bf16[512,768]{1,0:T(8,128)(2,1)} all-gather(bf16[128,768]{1,0:T(8,128)(2,1)S(1)} %bitcast.104), channel_id=1, replica_groups=mesh['dp'=4,'gx'=4,'gy'=2] {'gx'}, dimensions={0}, use_global_device_ids=true | all-gather | bytes 983040 | tf_op jit(solution)/shard_map/all_gather | solution.py:31
  148.8 2.0 reduce-scatter.10.cloned.1.call-done
  150.8 1.1 multiply_reduce_fusion
  151.8 1.0 multiply_convert_fusion.2
  152.9 18.3 %all_gather.55 = bf16[512,768]{1,0:T(8,128)(2,1)} all-gather(bf16[128,768]{1,0:T(8,128)(2,1)S(1)} %multiply_convert_fusion.2), channel_id=1, replica_groups=mesh['dp'=4,'gx'=4,'gy'=2] {'gx'}, dimensions={0}, use_global_device_ids=true | all-gather | bytes 983040 | tf_op jit(solution)/shard_map/all_gather | solution.py:31
  171.1 2.8 fusion.115
  174.0 2.1 fusion.10
  177.0 1.9 convolution_convert_fusion.2
  179.0 23.3 %reduce-scatter.14.cloned.1.call-done = bf16[128,768]{1,0:T(8,128)(2,1)} async-done(((bf16[512,768]{1,0:T(8,128)(2,1)}), bf16[128,768]{1,0:T(8,128)(2,1)}) %reduce-scatter.14.cloned.1.call-update) | async-done | bytes 196624 | tf_op jit(solution)/shard_map/reduce_scatter | solution.py:35
  202.4 1.2 fusion.35
  203.6 1.2 fusion.77
  204.8 18.2 %all_gather.58 = bf16[512,768]{1,0:T(8,128)(2,1)S(1)} all-gather(bf16[128,768]{1,0:T(8,128)(2,1)S(1)} %fusion.77), channel_id=1, replica_groups=mesh['dp'=4,'gx'=4,'gy'=2] {'gx'}, dimensions={0}, use_global_device_ids=true | all-gather | bytes 983040 | tf_op jit(solution)/shard_map/all_gather | solution.py:31
  224.0 1.4 convolution_convert_fusion.14
  225.5 5.8 %cross_backward.1 = (bf16[512,192]{1,0:T(8,128)(2,1)S(1)}, bf16[2,384,512]{2,1,0:T(8,128)(2,1)S(1)}) custom-call(bf16[512,192]{1,0:T(8,128)(2,1)S(1)} %convolution_convert_fusion.12.q_ref, bf16[2,512,384]{2,1,0:T(8,128)(2,1)S(1)} %bitcast.97, bf16[512,192]{1,0:T(8,128)(2,1)S(1)} %copy.101.dc_ref), custom_call_target="tpu_custom_call" | custom-call | tf_op jit(solution)/shard_map/cross_backward/pallas_call | solution.py:211
  232.2 2.2 convolution_convert_fusion.1
  234.5 2.9 convolution_convert_fusion
  237.4 1.2 convolution_convert_fusion.8
  239.1 2.8 convolution_convert_fusion.3
  242.0 2.4 add_convert_fusion.2
  244.4 1.9 reshape.235
  246.3 2.2 fusion.11
  249.5 1.1 pad_maximum_fusion
  254.5 1.1 convolution_convert_fusion.10
  255.8 1.5 convolution_convert_fusion.6
  257.4 1.2 fusion.36
  258.6 24.0 %reduce-scatter.12.cloned.1.call-done = bf16[128,768]{1,0:T(8,128)(2,1)} async-done(((bf16[512,768]{1,0:T(8,128)(2,1)}), bf16[128,768]{1,0:T(8,128)(2,1)}) %reduce-scatter.12.cloned.1.call-update) | async-done | bytes 196624 | tf_op jit(solution)/shard_map/reduce_scatter | solution.py:35
  282.6 2.0 fusion.109
  284.6 25.1 %all_gather.59 = bf16[512,768]{1,0:T(8,128)(2,1)S(1)} all-gather(bf16[128,768]{1,0:T(8,128)(2,1)S(1)} %get-tuple-element.42), channel_id=1, replica_groups=mesh['dp'=4,'gx'=4,'gy'=2] {'gx'}, dimensions={0}, use_global_device_ids=true | all-gather | bytes 983040 | tf_op jit(solution)/shard_map/all_gather | solution.py:31
  310.5 1.4 convolution_convert_fusion.13
  312.0 7.7 %self_backward.1 = (bf16[512,192]{1,0:T(8,128)(2,1)S(1)}, bf16[2,384,512]{2,1,0:T(8,128)(2,1)S(1)}, f32[8,1024]{1,0:T(8,128)S(1)}) custom-call(s32[1]{0:T(128)} %bitcast.2.core_ref, bf16[512,192]{1,0:T(8,128)(2,1)S(1)} %slice.140.q_ref, bf16[2,512,384]{2,1,0:T(8,128)(2,1)S(1)} %bitcast.95, s32[512,1]{1,0:T(8,128)S(1)} %copy.94.dq_ref, ...), custom_call_target="tpu_custom_call" | custom-call | tf_op jit(solution)/shard_map/self_backward/pallas_call | solution.py:211
  319.9 2.1 fusion.2
  322.5 1.5 add_convert_fusion.1
  324.0 1.9 pad_maximum_fusion.7
  330.6 4.5 %gather_fusion.1 = s32[1024]{0:T(1024)S(1)} fusion(s32[1024]{0:T(1024)S(1)} %copy-done.5, s32[1024]{0:T(1024)S(1)} %broadcast_clamp_fusion), kind=kCustom, calls=%fused_computation.1 | custom fusion | bytes 12288 | tf_op jit(solution)/shard_map/gather | solution.py:301
  335.2 4.7 %all_to_all.81 = bf16[128,2,384]{2,0,1:T(8,128)(2,1)} all-to-all(bf16[128,2,384]{2,0,1:T(8,128)(2,1)S(1)} %bitcast.117), channel_id=1, replica_groups=mesh['dp'=4,'gx'=4,'gy'=2] {'gy'}, dimensions={1} | all-to-all | bytes 393216 | tf_op jit(solution)/shard_map/all_to_all | solution.py:275
  341.2 4.8 %all_to_all.82 = f32[128,2,384]{2,0,1:T(8,128)} all-to-all(f32[128,2,384]{2,0,1:T(8,128)S(1)} %bitcast.112), channel_id=1, replica_groups=mesh['dp'=4,'gx'=4,'gy'=2] {'gy'}, dimensions={1} | all-to-all | bytes 786432 | tf_op jit(solution)/shard_map/all_to_all | solution.py:275
  346.0 3.2 reduce-scatter.18.cloned.1.call-done
  349.2 1.2 fusion.37
  350.4 1.1 fusion.28
  351.5 4.0 all_to_all.83
  355.6 39.5 %all-reduce = (f32[3,768]{1,0:T(4,128)}, f32[32,12]{0,1:T(8,128)}) all-reduce(f32[3,768]{1,0:T(4,128)S(1)} %pad_maximum_fusion.12, f32[32,12]{0,1:T(8,128)S(1)} %dynamic_update_slice.3), channel_id=1, replica_groups=mesh['dp'=4,'gx'=4,'gy'=2] {'dp','gx','gy'}, use_global_device_ids=true, to_apply=%region_16.17 | all-reduce | flops 2688 | bytes 21504 | tf_op jit(solution)/shard_map/psum | solution.py:445
  395.1 33.0 %all-reduce.4.cloned.1.call-done = (bf16[384,576]{0,1:T(8,128)(2,1)}, bf16[192,384]{1,0:T(8,128)(2,1)}, bf16[384,576]{0,1:T(8,128)(2,1)}, bf16[192,384]{1,0:T(8,128)(2,1)}, bf16[589824]{0:T(1024)(128)(2,1)}) async-done(((bf16[384,576]{0,1:T(8,128)(2,1)}, bf16[192,384]{1,0:T(8,128)(2,1)}, bf16[384,576]{0,1:T(8,128)(2,1)}, bf16[192,384]{1,0:T(8,128)(2,1)}, bf16[589824]{0:T(1024)(128)(2,1)}), ...) | async-done | bytes 2359312 | tf_op jit(solution)/shard_map/psum | solution.py:366
  428.0 2.5 slice.159
  430.6 1.5 slice.131
  432.1 1.3 fusion.111
  433.4 1.1 slice.135
  (226 shorter events, 27.8 us)
Async XLA Ops:
  7.2 38.2 %copy-start = (f32[32,12]{0,1:T(8,128)S(1)}, f32[32,12]{0,1:T(8,128)}, u32[]{:S(2)}) copy-start(f32[32,12]{0,1:T(8,128)} %param.22) | copy-start | bytes 4612
  7.2 5.6 %all-to-all-start = ((bf16[2,128,384]{2,1,0:T(8,128)(2,1)}), bf16[2,128,384]{2,1,0:T(8,128)(2,1)S(1)}, u32[]{:S(2)}, u32[]{:S(2)}) async-start(bf16[2,128,384]{2,1,0:T(8,128)(2,1)} %bitcast.121), calls=%async_computation | async-start | bytes 393216 | tf_op jit(solution)/shard_map/all_to_all | solution.py:272
  10.6 2.3 copy-start.51
  10.7 40.2 %all-gather.5.cloned.1.call-start = ((), (), s32[]{:S(2)}) async-start(), calls=%async_computation.12 | async-start | bytes 2064384 | tf_op jit(solution)/shard_map/all_gather | solution.py:286
  12.8 21.7 %copy-start.43 = (bf16[384,192]{0,1:T(8,128)(2,1)S(1)}, bf16[384,192]{0,1:T(8,128)(2,1)}, u32[]{:S(2)}) copy-start(bf16[384,192]{0,1:T(8,128)(2,1)} %param.26) | copy-start | bytes 442372
  12.8 21.7 %copy-start.44 = (bf16[384,192]{0,1:T(8,128)(2,1)S(1)}, bf16[384,192]{0,1:T(8,128)(2,1)}, u32[]{:S(2)}) copy-start(bf16[384,192]{0,1:T(8,128)(2,1)} %param.25) | copy-start | bytes 442372
  12.8 21.7 %copy-start.45 = (bf16[384,192]{0,1:T(8,128)(2,1)S(1)}, bf16[384,192]{0,1:T(8,128)(2,1)}, u32[]{:S(2)}) copy-start(bf16[384,192]{0,1:T(8,128)(2,1)} %param.24) | copy-start | bytes 442372
  12.8 78.8 %reduce-scatter.8.cloned.1.call-start = ((), (), s32[]{:S(2)}) async-start(), calls=%async_computation.13 | async-start | bytes 983040 | tf_op jit(solution)/shard_map/reduce_scatter | solution.py:35
  12.9 21.6 %copy-start.8 = (f32[2,16,8,384]{3,2,0,1:T(8,128)}, f32[2,16,8,384]{3,2,0,1:T(8,128)S(1)}, u32[]{:S(2)}) copy-start(f32[2,16,8,384]{3,2,0,1:T(8,128)S(1)} %copy.113) | copy-start | bytes 1179652
  34.5 3.3 copy-start.10
  45.6 7.6 %copy-start.41 = (bf16[1,256,384]{2,1,0:T(8,128)(2,1)S(1)}, bf16[1,256,384]{2,1,0:T(8,128)(2,1)}, u32[]{:S(2)}) copy-start(bf16[1,256,384]{2,1,0:T(8,128)(2,1)} %param.35) | copy-start | bytes 589828
  45.6 7.6 %copy-start.42 = (bf16[1,256,384]{2,1,0:T(8,128)(2,1)S(1)}, bf16[1,256,384]{2,1,0:T(8,128)(2,1)}, u32[]{:S(2)}) copy-start(bf16[1,256,384]{2,1,0:T(8,128)(2,1)} %param.19) | copy-start | bytes 589828
  53.1 97.6 %reduce-scatter.10.cloned.1.call-start = ((), (), s32[]{:S(2)}) async-start(), calls=%async_computation.14 | async-start | bytes 983040 | tf_op jit(solution)/shard_map/reduce_scatter | solution.py:35
  53.7 4.9 %copy-start.46 = (bf16[384,192]{0,1:T(8,128)(2,1)S(1)}, bf16[384,192]{0,1:T(8,128)(2,1)}, u32[]{:S(2)}) copy-start(bf16[384,192]{0,1:T(8,128)(2,1)} %param.30) | copy-start | bytes 442372
  53.7 4.9 %copy-start.47 = (bf16[384,192]{0,1:T(8,128)(2,1)S(1)}, bf16[384,192]{0,1:T(8,128)(2,1)}, u32[]{:S(2)}) copy-start(bf16[384,192]{0,1:T(8,128)(2,1)} %param.29) | copy-start | bytes 442372
  53.7 4.9 %copy-start.48 = (bf16[384,192]{0,1:T(8,128)(2,1)S(1)}, bf16[384,192]{0,1:T(8,128)(2,1)}, u32[]{:S(2)}) copy-start(bf16[384,192]{0,1:T(8,128)(2,1)} %param.28) | copy-start | bytes 442372
  61.1 28.0 %copy-start.33 = (bf16[768,576]{0,1:T(8,128)(2,1)}, bf16[768,576]{0,1:T(8,128)(2,1)S(1)}, u32[]{:S(2)}) copy-start(bf16[768,576]{0,1:T(8,128)(2,1)S(1)} %all_gather.51) | copy-start | bytes 2654212
  92.7 110.8 %copy-start.6 = (f32[128,768]{1,0:T(8,128)}, f32[128,768]{1,0:T(8,128)S(1)}, u32[]{:S(2)}) copy-start(f32[128,768]{1,0:T(8,128)S(1)} %get-tuple-element.45) | copy-start | bytes 1179652
  118.3 52.8 %all-gather.7.cloned.1.call-start = ((), (), s32[]{:S(2)}) async-start(), calls=%async_computation.15 | async-start | bytes 2359296 | tf_op jit(solution)/shard_map/all_gather | solution.py:285
  120.4 81.9 %reduce-scatter.14.cloned.1.call-start = ((), (), s32[]{:S(2)}) async-start(), calls=%async_computation.17 | async-start | bytes 983040 | tf_op jit(solution)/shard_map/reduce_scatter | solution.py:35
  171.1 2.8 copy-start.37
  171.1 2.8 copy-start.40
  173.9 3.1 copy-start.52
  177.0 25.3 %copy-start.12 = (bf16[128,768]{1,0:T(8,128)(2,1)S(1)}, bf16[128,768]{1,0:T(8,128)(2,1)}, u32[]{:S(2)}) copy-start(bf16[128,768]{1,0:T(8,128)(2,1)} %reduce-scatter.10.cloned.1.call-done) | copy-start | bytes 589828
  179.0 78.4 %reduce-scatter.16.cloned.1.call-start = ((), (), s32[]{:S(2)}) async-start(), calls=%async_computation.18 | async-start | bytes 983040 | tf_op jit(solution)/shard_map/reduce_scatter | solution.py:35
  234.4 48.2 %reduce-scatter.12.cloned.1.call-start = ((), (), s32[]{:S(2)}) async-start(), calls=%async_computation.16 | async-start | bytes 983040 | tf_op jit(solution)/shard_map/reduce_scatter | solution.py:35
  234.4 3.0 copy-start.38
  234.4 2.9 copy-start.53
  237.4 8.9 %collective-permute-start.8 = (bf16[384,1024]{1,0:T(8,128)(2,1)}, bf16[384,1024]{1,0:T(8,128)(2,1)}, u32[]{:S(2)}, u32[]{:S(2)}) collective-permute-start(bf16[384,1024]{1,0:T(8,128)(2,1)} %convolution_convert_fusion), channel_id=1, source_target_pairs={{0,1},{1,0},{2,3},{3,2},{4,5},{5,4},{6,7},{7,6},{8,9},{9,8},{10,11... | collective-permute-start | bytes 2359304 | tf_op jit(solution)/shard_map/ppermute | solution.py:42
  238.6 3.4 collective-permute-start.9
  241.9 98.3 %reduce-scatter.20.cloned.1.call-start = ((), (), s32[]{:S(2)}) async-start(), calls=%async_computation.20 | async-start | bytes 983040 | tf_op jit(solution)/shard_map/reduce_scatter | solution.py:35
  248.7 2.0 copy-start.23
  249.5 1.6 copy-start.21
  249.5 2.4 copy-start.3
  251.0 1.4 collective-permute-start.7
  251.4 1.9 collective-permute-start.5
  252.0 2.5 copy-start.18
  252.0 2.4 collective-permute-start.1
  253.3 2.4 copy-start.34
  255.6 1.8 copy-start.7
  255.6 27.0 %copy-start.13 = (bf16[128,768]{1,0:T(8,128)(2,1)S(1)}, bf16[128,768]{1,0:T(8,128)(2,1)}, u32[]{:S(2)}) copy-start(bf16[128,768]{1,0:T(8,128)(2,1)} %reduce-scatter.10.cloned.1.call-done) | copy-start | bytes 589828
  255.6 27.0 %copy-start.27 = (bf16[16,8,2,384]{3,1,2,0:T(8,128)(2,1)S(1)}, bf16[16,8,2,384]{3,1,2,0:T(8,128)(2,1)}, u32[]{:S(2)}) copy-start(bf16[16,8,2,384]{3,1,2,0:T(8,128)(2,1)} %copy-done.26) | copy-start | bytes 589828
  255.6 27.0 %copy-start.30 = (bf16[128,768]{1,0:T(8,128)(2,1)S(1)}, bf16[128,768]{1,0:T(8,128)(2,1)}, u32[]{:S(2)}) copy-start(bf16[128,768]{1,0:T(8,128)(2,1)} %reduce-scatter.14.cloned.1.call-done) | copy-start | bytes 589828
  255.6 64.3 %collective-permute-start.6 = (bf16[384,384]{1,0:T(8,128)(2,1)}, bf16[384,384]{1,0:T(8,128)(2,1)}, u32[]{:S(2)}, u32[]{:S(2)}) collective-permute-start(bf16[384,384]{1,0:T(8,128)(2,1)} %convolution_convert_fusion.10), channel_id=1, source_target_pairs={{0,1},{1,0},{2,3},{3,2},{4,5},{5,4},{6,7},{7,6},{8,9},{9,8},{10,11... | collective-permute-start | bytes 884744 | tf_op jit(solution)/shard_map/ppermute | solution.py:42
  257.3 91.9 %reduce-scatter.18.cloned.1.call-start = ((), (), s32[]{:S(2)}) async-start(), calls=%async_computation.19 | async-start | bytes 983040 | tf_op jit(solution)/shard_map/reduce_scatter | solution.py:35
  312.0 7.9 %copy-start.19 = (bf16[512,768]{1,0:T(8,128)(2,1)S(1)}, bf16[512,768]{1,0:T(8,128)(2,1)}, u32[]{:S(2)}) copy-start(bf16[512,768]{1,0:T(8,128)(2,1)} %copy-done.17) | copy-start | bytes 2359300
  312.0 10.0 %copy-start.16 = (bf16[768,576]{0,1:T(8,128)(2,1)S(1)}, bf16[768,576]{0,1:T(8,128)(2,1)}, u32[]{:S(2)}) copy-start(bf16[768,576]{0,1:T(8,128)(2,1)} %copy-done.15) | copy-start | bytes 2654212
  319.8 2.5 collective-permute-start
  322.5 1.6 copy-start.39
  324.0 2.0 copy-start.25
  324.0 2.8 copy-start.11
  324.0 104.1 %all-reduce.4.cloned.1.call-start = ((), (), s32[]{:S(2)}) async-start(), calls=%async_computation.21 | async-start | bytes 4718592 | tf_op jit(solution)/shard_map/psum | solution.py:366
  326.2 1.9 collective-permute-start.4
  327.1 2.0 collective-permute-start.2
  327.6 1.8 collective-permute-start.3
  330.6 4.6 %copy-start.35 = (bf16[128,768]{1,0:T(8,128)(2,1)S(1)}, bf16[128,768]{1,0:T(8,128)(2,1)}, u32[]{:S(2)}) copy-start(bf16[128,768]{1,0:T(8,128)(2,1)} %get-tuple-element.51) | copy-start | bytes 589828
  335.2 14.1 %copy-start.9 = (f32[2,16,8,384]{3,2,0,1:T(8,128)S(1)}, f32[2,16,8,384]{3,2,0,1:T(8,128)}, u32[]{:S(2)}) copy-start(f32[2,16,8,384]{3,2,0,1:T(8,128)} %copy-done.8) | copy-start | bytes 1179652
  428.0 2.5 copy-start.14
  433.4 2.0 copy-start.28
  434.5 1.9 copy-start.50
  434.5 2.6 copy-start.49
  435.4 2.4 copy-start.36
  435.4 3.8 copy-start.31
  435.4 4.6 %copy-start.1 = (f32[32,12]{0,1:T(8,128)S(1)}, f32[32,12]{0,1:T(8,128)}, u32[]{:S(2)}) copy-start(f32[32,12]{0,1:T(8,128)} %param.22) | copy-start | bytes 4612
  (13 other events, 12.5 us)
Sparse Core Ops, SparseCore 0:
  13.6 12.2 all-gather.4
  53.3 31.0 reduce-scatter.7
  118.4 32.2 reduce-scatter.9
  152.7 9.0 all-gather.6
  179.1 23.2 reduce-scatter.13
  234.5 22.5 reduce-scatter.15
  260.0 22.5 reduce-scatter.11
  285.4 28.9 reduce-scatter.19
  324.1 25.0 reduce-scatter.17
  353.2 74.7 all-reduce.3
